TPU v7x, 32 devices: a whole 2x2x4 slice. The times are simulated.
32 devices in a mesh: grp: 2 (over y), sx: 4 (over z), sy: 4 (over x, core).
Axes of the slice: x: 2, y: 2, z: 4, core: 2. Of those that a mesh axis runs over, the one named last changes fastest.
Arguments:
- field: float32 [4, 128, 96, 128], P('grp', 'sx', 'sy'), parts along dimension 0, may hold values from -6 to 6
- factor_x: float32 [128, 96], P('sx'), may hold values from -0.75 to 0.75
- factor_y: float32 [96, 64], P('sy'), may hold values from -0.875 to 0.875
- factor_z: float32 [128, 32], replicated, may hold values from -0.75 to 0.75
Outputs:
- core: float32 [4, 96, 2048], P('grp', None, ('sx', 'sy')), parts along dimension 0
- residual: float32 [4, 128, 96, 128], P('grp', 'sx', 'sy'), parts along dimension 0
There are 2 independent parts, one for each index of `grp`. A program takes and returns all parts, laid end to end along the dimension named above; an argument that names none is the same for every part. Nothing has to cross between parts.
All inputs are finite; a program needn't handle non-finite values.
Results may differ from a plain program's by a relative error of at most 0.000071.
Values sent between devices are 32-bit elements; how exact they have to be, the bound alone decides.
A program may use at most 64 MiB of HBM per device.

v0:
```python
import jax
import jax.numpy as jnp
from jax import lax
from jax.sharding import PartitionSpec as P


def local(field, factor_x, factor_y, factor_z):
    highest = lax.Precision.HIGHEST
    inner = jnp.einsum("sxyz,zc->sxyc", field, factor_z, precision=highest)
    inner = jnp.einsum("sxyc,yb->sxbc", inner, factor_y, precision=highest)
    snaps = inner.shape[0]
    rank_one = factor_x.shape[1]
    rank_two = inner.shape[2]
    rank_three = inner.shape[3]
    flat_width = rank_two * rank_three
    partial_core = jnp.einsum("sxbc,xa->sabc", inner, factor_x, precision=highest)
    flat_terms = partial_core.reshape(snaps, rank_one, flat_width)
    core_slice = lax.psum_scatter(flat_terms, ("sx", "sy"), scatter_dimension=2, tiled=True)
    whole_core = lax.all_gather(core_slice, ("sx", "sy"), axis=2, tiled=True)
    kernel = whole_core.reshape(snaps, rank_one, rank_two, rank_three)
    outer = jnp.einsum("sabc,xa->sxbc", kernel, factor_x, precision=highest)
    outer = jnp.einsum("sxbc,yb->sxyc", outer, factor_y, precision=highest)
    outer = jnp.einsum("sxyc,zc->sxyz", outer, factor_z, precision=highest)
    return (core_slice, field - outer)


def solution(mesh):
    in_specs = (P("grp", "sx", "sy", None), P("sx", None), P("sy", None), P())
    out_specs = (P("grp", None, ("sx", "sy")), P("grp", "sx", "sy", None))
    return jax.shard_map(local, mesh=mesh, in_specs=in_specs, out_specs=out_specs, check_vma=False)
```

profile of v0, /device:TPU:0, one launch (start us, length us, event | category | flops | bytes accessed | tf_op | source)
XLA Modules:
  0.0 142.2 jit_solution(17908177012130009558)
XLA Ops:
  7.2 0.0 copy-start
  7.2 0.0 copy-start.3
  7.2 0.0 reduce-scatter.2.cloned.1.call-start
  7.2 1.9 %fusion.1 = f32[2,32,24,32]{3,2,1,0:T(8,128)S(1)} fusion(f32[2,32,24,128]{3,2,1,0:T(8,128)} %param.4, f32[128,32]{0,1:T(8,128)} %param.7), kind=kOutput, calls=%fused_computation.6 | convolution fusion | flops 75497472 | bytes 999424 | tf_op jit(solution)/shard_map/sxyz,zc->sxyc/dot_general | solution.py:9
  9.1 0.3 copy.9
  9.5 0.0 copy-done.3
  9.5 1.8 %convolution_bitcast_fusion.2 = f32[2,32,64,32]{2,1,3,0:T(8,128)S(1)} fusion(f32[2,32,24,32]{1,2,3,0:T(8,128)S(1)} %copy.9, f32[24,64]{1,0:T(8,128)S(1)} %copy-done.3), kind=kOutput, calls=%fused_computation.2 | convolution fusion | flops 37748736 | bytes 727040 | tf_op jit(solution)/shard_map/sxyc,yb->sxbc/dot_general | solution.py:10
  11.3 0.0 copy-done
  11.4 3.5 %convolution_bitcast_fusion.1 = f32[2,96,64,32]{1,2,3,0:T(8,128)S(1)} fusion(f32[2,32,64,32]{2,1,3,0:T(8,128)S(1)} %convolution_bitcast_fusion.2, f32[32,96]{1,0:T(8,128)S(1)} %copy-done), kind=kOutput, calls=%fused_computation.1 | convolution fusion | flops 150994944 | bytes 2109440 | tf_op jit(solution)/shard_map/sxbc,xa->sabc/dot_general | solution.py:16
  14.9 2.6 %copy.6 = f32[2,96,64,32]{1,3,2,0:T(8,128)} copy(f32[2,96,64,32]{1,2,3,0:T(8,128)S(1)} %convolution_bitcast_fusion.1) | data formatting | bytes 3145728 | tf_op jit(solution)/shard_map/sxbc,xa->sabc/transpose | solution.py:16
  17.4 0.0 reduce-scatter.2.cloned.1.call-update
  17.4 0.2 all-gather.2.cloned.1.call-start
  17.7 64.2 %reduce-scatter.2.cloned.1.call-done = f32[2,96,128]{1,2,0:T(8,128)} async-done(((f32[2,96,2048]{1,2,0:T(8,128)}), f32[2,96,128]{1,2,0:T(8,128)}) %reduce-scatter.2.cloned.1.call-update) | async-done | bytes 98320 | tf_op jit(solution)/shard_map/reduce_scatter | solution.py:18
  81.9 0.0 all-gather.2.cloned.1.call-update
  81.9 1.6 %copy.7 = f32[2,96,128]{2,1,0:T(8,128)} copy(f32[2,96,128]{1,2,0:T(8,128)} %reduce-scatter.2.cloned.1.call-done) | data formatting | bytes 196608
  83.5 41.1 %all-gather.2.cloned.1.call-done = f32[2,96,2048]{1,2,0:T(8,128)} async-done(((f32[2,96,128]{1,2,0:T(8,128)}), f32[2,96,2048]{1,2,0:T(8,128)}) %all-gather.2.cloned.1.call-update) | async-done | bytes 1572880 | tf_op jit(solution)/shard_map/all_gather | solution.py:19
  124.7 3.4 %convolution_bitcast_fusion = f32[2,32,64,32]{1,3,2,0:T(8,128)S(1)} fusion(f32[2,96,64,32]{1,3,2,0:T(8,128)} %bitcast.38, f32[32,96]{1,0:T(8,128)S(1)} %copy-done), kind=kOutput, calls=%fused_computation | convolution fusion | flops 150994944 | bytes 2109440 | tf_op jit(solution)/shard_map/sabc,xa->sxbc/dot_general | solution.py:21
  128.0 0.0 copy-start.2
  128.1 1.5 %copy.12 = f32[2,32,64,32]{2,3,1,0:T(8,128)S(1)} copy(f32[2,32,64,32]{1,3,2,0:T(8,128)S(1)} %convolution_bitcast_fusion) | data formatting | bytes 1048576 | tf_op jit(solution)/shard_map/sabc,xa->sxbc/transpose | solution.py:21
  129.5 0.0 copy-start.1
  129.6 4.2 %convolution_bitcast_fusion.3 = f32[2,32,24,32]{3,2,1,0:T(8,128)S(1)} fusion(f32[2,32,64,32]{2,3,1,0:T(8,128)S(1)} %copy.12, f32[24,64]{1,0:T(8,128)S(1)} %copy-done.3), kind=kOutput, calls=%fused_computation.4 | convolution fusion | flops 37748736 | bytes 727040 | tf_op jit(solution)/shard_map/sxbc,yb->sxyc/dot_general | solution.py:22
  133.7 0.0 copy-done.2
  133.7 0.0 copy-done.1
  133.8 1.6 %convolution_subtract_fusion = f32[2,32,24,128]{3,2,1,0:T(8,128)} fusion(f32[2,32,24,128]{3,2,1,0:T(8,128)S(1)} %copy-done.1, f32[2,32,24,32]{3,2,1,0:T(8,128)S(1)} %convolution_bitcast_fusion.3, f32[128,32]{0,1:T(8,128)S(1)} %copy-done.2), kind=kOutput, calls=%fused_computation.3 | convolution fusion | flops 75694080 | bytes 1785856 | tf_op jit(solution)/shard_map/sxyc,zc->sxyz/dot_general | solution.py:23
Async XLA Ops:
  7.2 4.2 %copy-start = (f32[32,96]{1,0:T(8,128)S(1)}, f32[32,96]{1,0:T(8,128)}, u32[]{:S(2)}) copy-start(f32[32,96]{1,0:T(8,128)} %param.5) | copy-start | bytes 36868
  7.2 2.3 %copy-start.3 = (f32[24,64]{1,0:T(8,128)S(1)}, f32[24,64]{1,0:T(8,128)}, u32[]{:S(2)}) copy-start(f32[24,64]{1,0:T(8,128)} %param.6) | copy-start | bytes 18436
  7.2 74.7 %reduce-scatter.2.cloned.1.call-start = ((), (), s32[]{:S(2)}) async-start(), calls=%async_computation.1 | async-start | bytes 2228224 | tf_op jit(solution)/shard_map/reduce_scatter | solution.py:18
  17.4 107.2 %all-gather.2.cloned.1.call-start = ((), (), s32[]{:S(2)}) async-start(), calls=%async_computation.2 | async-start | bytes 2228224 | tf_op jit(solution)/shard_map/all_gather | solution.py:19
  128.0 5.7 %copy-start.2 = (f32[128,32]{0,1:T(8,128)S(1)}, f32[128,32]{0,1:T(8,128)}, u32[]{:S(2)}) copy-start(f32[128,32]{0,1:T(8,128)} %param.7) | copy-start | bytes 49156
  129.5 4.2 %copy-start.1 = (f32[2,32,24,128]{3,2,1,0:T(8,128)S(1)}, f32[2,32,24,128]{3,2,1,0:T(8,128)}, u32[]{:S(2)}) copy-start(f32[2,32,24,128]{3,2,1,0:T(8,128)} %param.4) | copy-start | bytes 2359300
Sparse Core Ops, SparseCore 0:
  17.6 64.2 reduce-scatter.1
  84.3 40.3 all-gather.1
where the time goes:
time: 142 us
  waiting for transfers between devices  105 us (74%)
  matrix products  16.4 us (12%)
  between operations  14.1 us (10%)
  local copies, waits for them, and re-layouts  6.07 us (4%)
    reduce_scatter x1, waiting for transfers between devices, local(): lax.psum_scatter(flat_terms, ('sx', 'sy'), scatter_dimension=2, tiled=True)  64.2 us
    all_gather x1, waiting for transfers between devices, local(): whole_core = lax.all_gather(core_slice, ('sx', 'sy'), axis=2, tiled=True)  41.1 us
    dot_general x1, matrix products, local(): outer = jnp.einsum('sxbc,yb->sxyc', outer, factor_y, precision=highest)  4.17 us
    dot_general x1, matrix products, local(): jnp.einsum('sxbc,xa->sabc', inner, factor_x, precision=highest)  3.49 us
    dot_general x1, matrix products, local(): outer = jnp.einsum('sabc,xa->sxbc', kernel, factor_x, precision=highest)  3.37 us
  transfers between devices with their start and end apart: 2, of which 2 were waited for; matrix products, arithmetic and copies ran while one was open for 1% of the time, Pallas kernels for 0%

commit v1 on v0

--- a/solution.py
+++ b/solution.py
@@ -1,10 +1,178 @@
+import functools
+
 import jax
 import jax.numpy as jnp
 from jax import lax
+from jax.experimental import pallas as pl
+from jax.experimental.pallas import tpu as pltpu
 from jax.sharding import PartitionSpec as P
 
-
-def local(field, factor_x, factor_y, factor_z):
+MESH = pl.DeviceIdType.MESH
+F32 = jnp.float32
+BF16 = jnp.bfloat16
+NN = (((1,), (0,)), ((), ()))
+NT = (((1,), (1,)), ((), ()))
+TN = (((0,), (0,)), ((), ()))
+
+
+def split(a):
+    high = a.astype(BF16)
+    return high, (a - high.astype(F32)).astype(BF16)
+
+
+def dot(a, b, dims=NN):
+    return lax.dot_general(a, b, dims, preferred_element_type=F32)
+
+
+def dot3(a, b, dims=NN):
+    return dot(a[0], b[0], dims) + (dot(a[0], b[1], dims) + dot(a[1], b[0], dims))
+
+
+def iota(shape, axis):
+    return lax.broadcasted_iota(jnp.int32, shape, axis)
+
+
+def exchange_segments(tiles):
+    segment = iota(tiles[0].shape, 1) // 32
+    a, b, c, d = tiles
+    low = segment < 2
+    a, c = jnp.where(low, a, pltpu.roll(c, 64, 1)), jnp.where(low, pltpu.roll(a, 64, 1), c)
+    b, d = jnp.where(low, b, pltpu.roll(d, 64, 1)), jnp.where(low, pltpu.roll(b, 64, 1), d)
+    even = segment % 2 == 0
+    a, b = jnp.where(even, a, pltpu.roll(b, 32, 1)), jnp.where(even, pltpu.roll(a, 96, 1), b)
+    c, d = jnp.where(even, c, pltpu.roll(d, 32, 1)), jnp.where(even, pltpu.roll(c, 96, 1), d)
+    return a, b, c, d
+
+
+def kernel(nsx, nsy, field, fx, fy, fz, core_out, res_out, ux, uy, bd_h, bd_l, send1, recv1, send2, recv2,
+           csend, crecv, ux_s, ux_r, uy_s, uy_r, s1_s, s1_r, s2_s, s2_r, c_s, c_r):
+    n = nsx * nsy
+    snaps, xl, yl, nz = field.shape
+    sx, sy = lax.axis_index("sx"), lax.axis_index("sy")
+    me = sx * nsy + sy
+
+    def peer(i):
+        q = lax.rem(me + i, n)
+        return q, {"sx": q // nsy, "sy": lax.rem(q, nsy)}
+
+    def send(src, dst, send_sems, recv_sems, i, device):
+        return pltpu.make_async_remote_copy(src_ref=src, dst_ref=dst, send_sem=send_sems.at[i], recv_sem=recv_sems.at[i],
+                                            device_id=device, device_id_type=MESH)
+
+    barrier = pltpu.get_barrier_semaphore()
+    for i in range(1, n):
+        pl.semaphore_signal(barrier, inc=1, device_id=peer(i)[1], device_id_type=MESH)
+
+    spread_r, spread_c = iota((32, 256), 0), iota((32, 256), 1)
+    spread = jnp.where((spread_c // 32 == spread_r // 4) & (spread_c % 4 == spread_r % 4), 1.0, 0.0).astype(BF16)
+    lane_x = (iota((nz, 256), 1) // 4) % 8
+    for ref, part in zip((bd_h, bd_l), split(fz[...])):
+        wide = dot(part, spread)
+        for j in range(8):
+            ref[j * nz:(j + 1) * nz, :] = jnp.where(lane_x == j, wide, 0.0).astype(BF16)
+    bd = (bd_h[...], bd_l[...])
+
+    pl.semaphore_wait(barrier, n - 1)
+
+    copies = []
+    for i in range(1, nsx):
+        copies.append(send(fx, ux.at[sx], ux_s, ux_r, i, {"sx": lax.rem(sx + i, nsx)}))
+    for i in range(1, nsy):
+        copies.append(send(fy, uy.at[sy], uy_s, uy_r, i, {"sy": lax.rem(sy + i, nsy)}))
+    for copy in copies:
+        copy.start()
+    ux[pl.ds(sx, 1)] = fx[...][None]
+    uy[pl.ds(sy, 1)] = fy[...][None]
+
+    xo = xl // 8
+    for s in range(snaps):
+        snap = field[s].reshape(xo, 8, yl, nz)
+        rows = jnp.concatenate([snap[:, j].reshape(xo * yl, nz) for j in range(8)], axis=1)
+        packed = dot3(split(rows), bd)
+        for t in range(2):
+            tiles = [packed[o * yl:(o + 1) * yl, t * 128:(t + 1) * 128] for o in range(xo)]
+            for k, tile in enumerate(exchange_segments(tiles)):
+                send1[s * 8 + t * 4 + k] = tile
+
+    first = []
+    for i in range(1, n):
+        q, device = peer(i)
+        first.append(send(send1.at[q], recv1.at[me], s1_s, s1_r, i, device))
+    for copy in first:
+        copy.start()
+    recv1[pl.ds(me, 1)] = send1[pl.ds(me, 1)]
+
+    for copy in copies:
+        copy.wait()
+    uy_all = uy[...].reshape(nsy * yl, uy.shape[2])
+    ux_all = ux[...].reshape(nsx * xl, ux.shape[2])
+    rank1, rank2 = ux_all.shape[1], uy_all.shape[1]
+    uy_p = split(uy_all)
+    eye = jnp.where(iota((rank2, rank2), 0) == iota((rank2, rank2), 1), 1.0, 0.0).astype(BF16)
+    left = jnp.concatenate([dot3(uy_p, uy_p, NT), dot(eye, uy_p[0], NT) + dot(eye, uy_p[1], NT)], axis=0)
+    left = split(left)
+    nx = nsx * xl
+    wide_x = 4 * nx
+    repeat = jnp.where(iota((wide_x, nx), 0) // 4 == iota((wide_x, nx), 1), 1.0, 0.0).astype(BF16)
+    ux_pad = jnp.concatenate([ux_all, jnp.zeros((nx, 128 - rank1), F32)], axis=1)
+    xe_f = [dot(repeat, part) for part in split(ux_pad)]
+    xe = [part.astype(BF16) for part in xe_f]
+    same = (iota((wide_x, wide_x), 0) % 4) == (iota((wide_x, wide_x), 1) % 4)
+    px = split(jnp.where(same, dot3(xe, xe, NT), 0.0))
+    row_c = iota((wide_x, 128), 0) % 4
+    wx = [jnp.concatenate([jnp.where(row_c == c, part, 0.0).astype(BF16) for c in range(4)], axis=1) for part in xe_f]
+
+    for copy in first:
+        copy.wait()
+    whole = jnp.concatenate([recv1[g * nsy:(g + 1) * nsy].reshape(nsy * yl, 128) for g in range(nsx)], axis=1)
+    both = dot3(left, split(whole))
+    back = dot3(split(both[:nsy * yl]), px)
+    for g in range(nsx):
+        send2[g * nsy:(g + 1) * nsy] = back[:, g * 128:(g + 1) * 128].reshape(nsy, yl, 128)
+    second = []
+    for i in range(1, n):
+        q, device = peer(i)
+        second.append(send(send2.at[q], recv2.at[me], s2_s, s2_r, i, device))
+    for copy in second:
+        copy.start()
+    recv2[pl.ds(me, 1)] = send2[pl.ds(me, 1)]
+
+    core = dot3(split(both[nsy * yl:]), wx)
+    for q in range(n):
+        for h in range(2):
+            csend[q, h * 4:(h + 1) * 4, :] = core[q * 4:(q + 1) * 4, h * 256:(h + 1) * 256]
+    third = []
+    for i in range(1, n):
+        q, device = peer(i)
+        third.append(send(csend.at[q], crecv.at[me], c_s, c_r, i, device))
+    for copy in third:
+        copy.start()
+    crecv[pl.ds(me, 1)] = csend[pl.ds(me, 1)]
+
+    for copy in second:
+        copy.wait()
+    for s in range(snaps):
+        halves = []
+        for t in range(2):
+            tiles = exchange_segments([recv2[s * 8 + t * 4 + k] for k in range(4)])
+            halves.append(jnp.concatenate(tiles, axis=0))
+        rebuilt = dot3(split(jnp.concatenate(halves, axis=1)), bd, NT)
+        for j in range(8):
+            for o in range(xo):
+                res_out[s, o * 8 + j] = field[s, o * 8 + j] - rebuilt[o * yl:(o + 1) * yl, j * nz:(j + 1) * nz]
+
+    for copy in third:
+        copy.wait()
+    k = iota((128, 128), 0)
+    lane = (k % 4) * 32 + ((k // 8) % 8) * 4 + ((k // 4) % 2) * 2 + k // 64
+    order = jnp.where(lane == iota((128, 128), 1), 1.0, 0.0).astype(BF16)
+    for s in range(snaps):
+        got = crecv[s * 8:(s + 1) * 8].reshape(64, 256)
+        high, low = split(jnp.concatenate([got[:, :128], got[:, 128:]], axis=0))
+        core_out[s] = (dot(high, order, TN) + dot(low, order, TN))[:rank1]
+
+
+def plain(field, factor_x, factor_y, factor_z):
     highest = lax.Precision.HIGHEST
     inner = jnp.einsum("sxyz,zc->sxyc", field, factor_z, precision=highest)
     inner = jnp.einsum("sxyc,yb->sxbc", inner, factor_y, precision=highest)
@@ -24,7 +192,41 @@
     return (core_slice, field - outer)
 
 
+def local(nsx, nsy, field, factor_x, factor_y, factor_z):
+    snaps, xl, yl, nz = field.shape
+    rank1, rank2, rank3 = factor_x.shape[1], factor_y.shape[1], factor_z.shape[1]
+    n = nsx * nsy
+    fits = (n == 16 and snaps == 2 and rank3 == 32 and xl == 32 and nz == 128 and yl % 24 == 0 and rank2 == 64
+            and rank1 <= 128 and rank1 % 8 == 0 and yl <= 64)
+    if not fits:
+        return plain(field, factor_x, factor_y, factor_z)
+    vmem = pl.BlockSpec(memory_space=pltpu.VMEM)
+    dma = pltpu.SemaphoreType.DMA
+    return pl.pallas_call(
+        functools.partial(kernel, nsx, nsy),
+        out_shape=(jax.ShapeDtypeStruct((snaps, rank1, rank2 * rank3 // n), F32), jax.ShapeDtypeStruct(field.shape, F32)),
+        in_specs=[vmem] * 4,
+        out_specs=(vmem, vmem),
+        scratch_shapes=[
+            pltpu.VMEM((nsx, xl, rank1), F32),
+            pltpu.VMEM((nsy, yl, rank2), F32),
+            pltpu.VMEM((8 * nz, 256), BF16),
+            pltpu.VMEM((8 * nz, 256), BF16),
+            pltpu.VMEM((n, yl, 128), F32),
+            pltpu.VMEM((n, yl, 128), F32),
+            pltpu.VMEM((n, yl, 128), F32),
+            pltpu.VMEM((n, yl, 128), F32),
+            pltpu.VMEM((n, 8, 256), F32),
+            pltpu.VMEM((n, 8, 256), F32),
+            dma((nsx,)), dma((nsx,)), dma((nsy,)), dma((nsy,)),
+            dma((n,)), dma((n,)), dma((n,)), dma((n,)), dma((n,)), dma((n,)),
+        ],
+        compiler_params=pltpu.CompilerParams(collective_id=0, has_side_effects=True, vmem_limit_bytes=40 * 2**20),
+    )(field, factor_x, factor_y, factor_z)
+
+
 def solution(mesh):
     in_specs = (P("grp", "sx", "sy", None), P("sx", None), P("sy", None), P())
     out_specs = (P("grp", None, ("sx", "sy")), P("grp", "sx", "sy", None))
-    return jax.shard_map(local, mesh=mesh, in_specs=in_specs, out_specs=out_specs, check_vma=False)
+    body = functools.partial(local, mesh.shape["sx"], mesh.shape["sy"])
+    return jax.shard_map(body, mesh=mesh, in_specs=in_specs, out_specs=out_specs, check_vma=False)

time: 142 us -> 27.7 us (0.20)
  waiting for transfers between devices: 105 us -> 0 us
  Pallas kernels: 0 us -> 23.3 us
  matrix products: 16.4 us -> 0 us
  between operations: 14.1 us -> 0.68 us
  local copies, waits for them, and re-layouts: 6.07 us -> 3.48 us
    reduce_scatter x1 -> x0, waiting for transfers between devices: 64.2 us -> none  [local(): lax.psum_scatter(flat_terms, ('sx', 'sy'), scatter_dimension=2, tiled=True)]
    all_gather x1 -> x0, waiting for transfers between devices: 41.1 us -> none  [local(): whole_core = lax.all_gather(core_slice, ('sx', 'sy'), axis=2, tiled=True)]
    pallas_call x0 -> x1, Pallas kernels: none -> 23.3 us  [local(): pl.pallas_call(functools.partial(kernel, nsx, nsy), out_shape=(jax.ShapeD...]
    dot_general x6 -> x0, matrix products: 16.4 us -> none  [the longest x1 4.17 us: local(): outer = jnp.einsum('sxbc,yb->sxyc', outer, factor_y, precision=highest)]
    transpose x2 -> x0, local copies, waits for them, and re-layouts: 4.05 us -> none  [the longest x1 2.57 us: local(): jnp.einsum('sxbc,xa->sabc', inner, factor_x, precision=highest)]
    unnamed x9, local copies, waits for them, and re-layouts: 1.66 us -> 3.48 us
  transfers between devices with their start and end apart: 2 -> 0, of which waited for: 2 -> 0; matrix products, arithmetic and copies ran while one was open for 1% -> 0% of each run, Pallas kernels for 0% -> 0%
where the time goes in v1:
time: 27.7 us; the launch traced here: 27.5 us
  Pallas kernels  23.3 us (84%)
  local copies, waits for them, and re-layouts  3.48 us (13%)
  between operations  0.68 us (2%)
    pallas_call x1, Pallas kernels, local(): pl.pallas_call(functools.partial(kernel, nsx, nsy), out_shape=(jax.ShapeD...  23.3 us
    unnamed x9, local copies, waits for them, and re-layouts  3.48 us

profile of v1, /device:TPU:0, one launch (start us, length us, event | category | flops | bytes accessed | tf_op | source)
XLA Modules:
  0.0 27.5 jit_solution(2941118678554236971)
XLA Ops:
  0.6 0.0 copy-start.2
  0.6 0.0 copy-start.1
  0.7 0.8 %copy.6.fz = f32[128,32]{1,0:T(8,128)S(1)} copy(f32[128,32]{0,1:T(8,128)} %param.7) | data formatting | bytes 32768 | tf_op args[3]
  1.5 0.0 copy-done.2
  1.5 0.0 copy-done.1
  1.5 0.0 copy-start
  1.5 1.1 %copy-done = f32[2,32,24,128]{3,2,1,0:T(8,128)S(1)} copy-done((f32[2,32,24,128]{3,2,1,0:T(8,128)S(1)}, f32[2,32,24,128]{3,2,1,0:T(8,128)}, u32[]{:S(2)}) %copy-start) | copy-done | bytes 786456
  2.6 23.3 %shard_map.59 = (f32[2,96,128]{2,1,0:T(8,128)S(1)}, f32[2,32,24,128]{3,2,1,0:T(8,128)S(1)}) custom-call(f32[2,32,24,128]{3,2,1,0:T(8,128)S(1)} %copy-done, f32[32,96]{1,0:T(8,128)S(1)} %copy-done.1, f32[24,64]{1,0:T(8,128)S(1)} %copy-done.2, f32[128,32]{1,0:T(8,128)S(1)} %copy.6.fz), custom_call_target="tpu_custom_call" | custom-call | tf_op jit(solution)/shard_map/pallas_call | solution.py:205
  26.0 0.6 %copy.9 = f32[2,96,128]{2,1,0:T(8,128)} copy(f32[2,96,128]{2,1,0:T(8,128)S(1)} %get-tuple-element.4) | data formatting | bytes 196608
  26.6 0.9 %copy.10 = f32[2,32,24,128]{3,2,1,0:T(8,128)} copy(f32[2,32,24,128]{3,2,1,0:T(8,128)S(1)} %get-tuple-element.5) | data formatting | bytes 1572864
Async XLA Ops:
  0.6 0.8 %copy-start.2 = (f32[24,64]{1,0:T(8,128)S(1)}, f32[24,64]{1,0:T(8,128)}, u32[]{:S(2)}) copy-start(f32[24,64]{1,0:T(8,128)} %fy.1) | copy-start | bytes 18436
  0.6 0.8 %copy-start.1 = (f32[32,96]{1,0:T(8,128)S(1)}, f32[32,96]{1,0:T(8,128)}, u32[]{:S(2)}) copy-start(f32[32,96]{1,0:T(8,128)} %fx.1) | copy-start | bytes 36868
  1.5 1.1 %copy-start = (f32[2,32,24,128]{3,2,1,0:T(8,128)S(1)}, f32[2,32,24,128]{3,2,1,0:T(8,128)}, u32[]{:S(2)}) copy-start(f32[2,32,24,128]{3,2,1,0:T(8,128)} %field.1) | copy-start | bytes 2359300

commit v2 on v1

--- a/solution.py
+++ b/solution.py
@@ -7,6 +7,8 @@
 from jax.experimental.pallas import tpu as pltpu
 from jax.sharding import PartitionSpec as P
 
+STOP = 0
+LIMIT = 40
 MESH = pl.DeviceIdType.MESH
 F32 = jnp.float32
 BF16 = jnp.bfloat16
@@ -44,8 +46,8 @@
     return a, b, c, d
 
 
-def kernel(nsx, nsy, field, fx, fy, fz, core_out, res_out, ux, uy, bd_h, bd_l, send1, recv1, send2, recv2,
-           csend, crecv, ux_s, ux_r, uy_s, uy_r, s1_s, s1_r, s2_s, s2_r, c_s, c_r):
+def kernel(nsx, nsy, stop, field_hbm, fx, fy, fz_hbm, recv2, crecv, field, bd_h, bd_l, ux, uy, fz, send1, recv1, send2,
+           csend, in_s, ux_s, ux_r, uy_s, uy_r, s1_s, s1_r, s2_s, s2_r, c_s, c_r):
     n = nsx * nsy
     snaps, xl, yl, nz = field.shape
     sx, sy = lax.axis_index("sx"), lax.axis_index("sy")
@@ -59,21 +61,39 @@
         return pltpu.make_async_remote_copy(src_ref=src, dst_ref=dst, send_sem=send_sems.at[i], recv_sem=recv_sems.at[i],
                                             device_id=device, device_id_type=MESH)
 
+    loads = [pltpu.make_async_copy(fz_hbm, fz, in_s.at[0])]
+    for s in range(snaps):
+        loads.append(pltpu.make_async_copy(field_hbm.at[s], field.at[s], in_s.at[1 + s]))
+    loads.append(pltpu.make_async_copy(fx, ux.at[sx], in_s.at[1 + snaps]))
+    loads.append(pltpu.make_async_copy(fy, uy.at[sy], in_s.at[2 + snaps]))
+    for load in loads:
+        load.start()
+
     barrier = pltpu.get_barrier_semaphore()
     for i in range(1, n):
         pl.semaphore_signal(barrier, inc=1, device_id=peer(i)[1], device_id_type=MESH)
 
+    if stop == 7:
+        pl.semaphore_wait(barrier, n - 1)
+        for load in loads:
+            load.wait()
+        return
     spread_r, spread_c = iota((32, 256), 0), iota((32, 256), 1)
     spread = jnp.where((spread_c // 32 == spread_r // 4) & (spread_c % 4 == spread_r % 4), 1.0, 0.0).astype(BF16)
+    loads[0].wait()
     lane_x = (iota((nz, 256), 1) // 4) % 8
     for ref, part in zip((bd_h, bd_l), split(fz[...])):
-        wide = dot(part, spread)
+        wide = dot(part, spread, TN)
         for j in range(8):
             ref[j * nz:(j + 1) * nz, :] = jnp.where(lane_x == j, wide, 0.0).astype(BF16)
     bd = (bd_h[...], bd_l[...])
 
     pl.semaphore_wait(barrier, n - 1)
 
+    if stop == 8:
+        for load in loads[1:]:
+            load.wait()
+        return
     copies = []
     for i in range(1, nsx):
         copies.append(send(fx, ux.at[sx], ux_s, ux_r, i, {"sx": lax.rem(sx + i, nsx)}))
@@ -81,11 +101,14 @@
         copies.append(send(fy, uy.at[sy], uy_s, uy_r, i, {"sy": lax.rem(sy + i, nsy)}))
     for copy in copies:
         copy.start()
-    ux[pl.ds(sx, 1)] = fx[...][None]
-    uy[pl.ds(sy, 1)] = fy[...][None]
+    if stop == 1:
+        for copy in copies + loads[1:]:
+            copy.wait()
+        return
 
     xo = xl // 8
     for s in range(snaps):
+        loads[1 + s].wait()
         snap = field[s].reshape(xo, 8, yl, nz)
         rows = jnp.concatenate([snap[:, j].reshape(xo * yl, nz) for j in range(8)], axis=1)
         packed = dot3(split(rows), bd)
@@ -94,6 +117,10 @@
             for k, tile in enumerate(exchange_segments(tiles)):
                 send1[s * 8 + t * 4 + k] = tile
 
+    if stop == 2:
+        for copy in copies + loads[1 + snaps:]:
+            copy.wait()
+        return
     first = []
     for i in range(1, n):
         q, device = peer(i)
@@ -102,7 +129,11 @@
         copy.start()
     recv1[pl.ds(me, 1)] = send1[pl.ds(me, 1)]
 
-    for copy in copies:
+    if stop == 3:
+        for copy in copies + loads[1 + snaps:] + first:
+            copy.wait()
+        return
+    for copy in copies + loads[1 + snaps:]:
         copy.wait()
     uy_all = uy[...].reshape(nsy * yl, uy.shape[2])
     ux_all = ux[...].reshape(nsx * xl, ux.shape[2])
@@ -124,11 +155,16 @@
 
     for copy in first:
         copy.wait()
+    if stop == 4:
+        ux[0:1, :, :] = (px[0][:32, :96].astype(F32) + wx[0][:32, :96].astype(F32) + left[0][:32, :96].astype(F32))[None]
+        return
     whole = jnp.concatenate([recv1[g * nsy:(g + 1) * nsy].reshape(nsy * yl, 128) for g in range(nsx)], axis=1)
     both = dot3(left, split(whole))
     back = dot3(split(both[:nsy * yl]), px)
     for g in range(nsx):
         send2[g * nsy:(g + 1) * nsy] = back[:, g * 128:(g + 1) * 128].reshape(nsy, yl, 128)
+    if stop == 5:
+        return
     second = []
     for i in range(1, n):
         q, device = peer(i)
@@ -137,6 +173,10 @@
         copy.start()
     recv2[pl.ds(me, 1)] = send2[pl.ds(me, 1)]
 
+    if stop == 6:
+        for copy in second:
+            copy.wait()
+        return
     core = dot3(split(both[nsy * yl:]), wx)
     for q in range(n):
         for h in range(2):
@@ -149,8 +189,16 @@
         copy.start()
     crecv[pl.ds(me, 1)] = csend[pl.ds(me, 1)]
 
-    for copy in second:
+    for copy in second + third:
         copy.wait()
+
+
+def finish(recv2, crecv, field, bd_h, bd_l, core_hbm, res_hbm, core_out, res_out, sems):
+    snaps, xl, yl, nz = field.shape
+    rank1 = core_out.shape[1]
+    xo = xl // 8
+    bd = (bd_h[...], bd_l[...])
+    stores = []
     for s in range(snaps):
         halves = []
         for t in range(2):
@@ -160,9 +208,9 @@
         for j in range(8):
             for o in range(xo):
                 res_out[s, o * 8 + j] = field[s, o * 8 + j] - rebuilt[o * yl:(o + 1) * yl, j * nz:(j + 1) * nz]
-
-    for copy in third:
-        copy.wait()
+        stores.append(pltpu.make_async_copy(res_out.at[s], res_hbm.at[s], sems.at[s]))
+        stores[-1].start()
+
     k = iota((128, 128), 0)
     lane = (k % 4) * 32 + ((k // 8) % 8) * 4 + ((k // 4) % 2) * 2 + k // 64
     order = jnp.where(lane == iota((128, 128), 1), 1.0, 0.0).astype(BF16)
@@ -170,6 +218,10 @@
         got = crecv[s * 8:(s + 1) * 8].reshape(64, 256)
         high, low = split(jnp.concatenate([got[:, :128], got[:, 128:]], axis=0))
         core_out[s] = (dot(high, order, TN) + dot(low, order, TN))[:rank1]
+    stores.append(pltpu.make_async_copy(core_out, core_hbm, sems.at[snaps]))
+    stores[-1].start()
+    for store in stores:
+        store.wait()
 
 
 def plain(field, factor_x, factor_y, factor_z):
@@ -202,27 +254,42 @@
         return plain(field, factor_x, factor_y, factor_z)
     vmem = pl.BlockSpec(memory_space=pltpu.VMEM)
     dma = pltpu.SemaphoreType.DMA
-    return pl.pallas_call(
-        functools.partial(kernel, nsx, nsy),
-        out_shape=(jax.ShapeDtypeStruct((snaps, rank1, rank2 * rank3 // n), F32), jax.ShapeDtypeStruct(field.shape, F32)),
-        in_specs=[vmem] * 4,
-        out_specs=(vmem, vmem),
+    hbm = pl.BlockSpec(memory_space=pltpu.HBM)
+    wide = (n, yl, 128)
+    passed = pl.pallas_call(
+        functools.partial(kernel, nsx, nsy, STOP),
+        out_shape=(
+            jax.ShapeDtypeStruct(wide, F32),
+            jax.ShapeDtypeStruct((n, 8, 256), F32),
+            jax.ShapeDtypeStruct(field.shape, F32),
+            jax.ShapeDtypeStruct((8 * nz, 256), BF16),
+            jax.ShapeDtypeStruct((8 * nz, 256), BF16),
+        ),
+        in_specs=[hbm] * 4,
+        out_specs=(vmem,) * 5,
         scratch_shapes=[
             pltpu.VMEM((nsx, xl, rank1), F32),
             pltpu.VMEM((nsy, yl, rank2), F32),
-            pltpu.VMEM((8 * nz, 256), BF16),
-            pltpu.VMEM((8 * nz, 256), BF16),
-            pltpu.VMEM((n, yl, 128), F32),
-            pltpu.VMEM((n, yl, 128), F32),
-            pltpu.VMEM((n, yl, 128), F32),
-            pltpu.VMEM((n, yl, 128), F32),
+            pltpu.VMEM((rank3, nz), F32),
+            pltpu.VMEM(wide, F32),
+            pltpu.VMEM(wide, F32),
+            pltpu.VMEM(wide, F32),
             pltpu.VMEM((n, 8, 256), F32),
-            pltpu.VMEM((n, 8, 256), F32),
+            dma((snaps + 3,)),
             dma((nsx,)), dma((nsx,)), dma((nsy,)), dma((nsy,)),
             dma((n,)), dma((n,)), dma((n,)), dma((n,)), dma((n,)), dma((n,)),
         ],
-        compiler_params=pltpu.CompilerParams(collective_id=0, has_side_effects=True, vmem_limit_bytes=40 * 2**20),
-    )(field, factor_x, factor_y, factor_z)
+        compiler_params=pltpu.CompilerParams(collective_id=0, has_side_effects=True, vmem_limit_bytes=LIMIT * 2**20),
+    )(*[pltpu.with_memory_space_constraint(v, pltpu.HBM) for v in (field, factor_x, factor_y, factor_z.T)])
+    core_shape = (snaps, rank1, rank2 * rank3 // n)
+    return pl.pallas_call(
+        finish,
+        out_shape=(jax.ShapeDtypeStruct(core_shape, F32), jax.ShapeDtypeStruct(field.shape, F32)),
+        in_specs=[vmem] * 5,
+        out_specs=(hbm, hbm),
+        scratch_shapes=[pltpu.VMEM(core_shape, F32), pltpu.VMEM(field.shape, F32), dma((snaps + 1,))],
+        compiler_params=pltpu.CompilerParams(vmem_limit_bytes=40 * 2**20),
+    )(*passed)
 
 
 def solution(mesh):

time: 27.7 us -> 26.4 us (0.953)
  local copies, waits for them, and re-layouts: 3.48 us -> 0 us
  Pallas kernels: 23.3 us -> 25.6 us
    unnamed x9 -> x0, local copies, waits for them, and re-layouts: 3.48 us -> none
    pallas_call x1 -> x2, Pallas kernels: 23.3 us -> 25.6 us  [the longest x1 23.6 us: local(): pl.pallas_call(functools.partial(kernel, nsx, nsy, STOP), out_shape=(jax....]
where the time goes in v2:
time: 26.4 us; the launch traced here: 26.2 us
  Pallas kernels  25.6 us (97%)
  between operations  0.64 us (2%)
    pallas_call x1, Pallas kernels, local(): pl.pallas_call(functools.partial(kernel, nsx, nsy, STOP), out_shape=(jax....  23.6 us
    pallas_call x1, Pallas kernels, local(): pl.pallas_call(finish, out_shape=(jax.ShapeDtypeStruct(core_shape, F32),...  2 us

profile of v2, /device:TPU:0, one launch (start us, length us, event | category | flops | bytes accessed | tf_op | source)
XLA Modules:
  0.0 26.2 jit_solution(16123625500843492558)
XLA Ops:
  0.6 23.6 %shard_map.59 = (f32[16,24,128]{2,1,0:T(8,128)S(1)}, f32[16,8,256]{2,1,0:T(8,128)S(1)}, f32[2,32,24,128]{3,2,1,0:T(8,128)S(1)}, bf16[1024,256]{1,0:T(8,128)(2,1)S(1)}, bf16[1024,256]{1,0:T(8,128)(2,1)S(1)}) custom-call(f32[2,32,24,128]{3,2,1,0:T(8,128)} %field_hbm.1, f32[32,96]{1,0:T(8,128)} %fx.1, f32[24,64]{1,0:T(8,128)} %fy.1, f32[32,128]{1,0:T(8,128)} %bitcast.1), custom_call_target="tpu_custom_call" | custom-call | tf_op jit(solution)/shard_map/pallas_call | solution.py:259
  24.2 2.0 %shard_map.60 = (f32[2,96,128]{2,1,0:T(8,128)}, f32[2,32,24,128]{3,2,1,0:T(8,128)}) custom-call(f32[16,24,128]{2,1,0:T(8,128)S(1)} %get-tuple-element.7.recv2, f32[16,8,256]{2,1,0:T(8,128)S(1)} %get-tuple-element.8.crecv, f32[2,32,24,128]{3,2,1,0:T(8,128)S(1)} %get-tuple-element.9.field, bf16[1024,256]{1,0:T(8,128)(2,1)S(1)} %get-tuple-element.10.bd_h, ...), custom_call_target="tpu_custom_call" | custom-call | tf_op jit(solution)/shard_map/pallas_call | solution.py:285

commit v3 on v2

v3 whole, which is shorter than its diff:
```python
import functools

import jax
import jax.numpy as jnp
from jax import lax
from jax.experimental import pallas as pl
from jax.experimental.pallas import tpu as pltpu
from jax.sharding import PartitionSpec as P

PARTS = 2
MESH = pl.DeviceIdType.MESH
F32 = jnp.float32
BF16 = jnp.bfloat16
NN = (((1,), (0,)), ((), ()))
NT = (((1,), (1,)), ((), ()))
TN = (((0,), (0,)), ((), ()))


def split(a):
    high = a.astype(BF16)
    return high, (a - high.astype(F32)).astype(BF16)


def dot(a, b, dims=NN):
    return lax.dot_general(a, b, dims, preferred_element_type=F32)


def dot3(a, b, dims=NN):
    return dot(a[0], b[0], dims) + (dot(a[0], b[1], dims) + dot(a[1], b[0], dims))


def iota(shape, axis):
    return lax.broadcasted_iota(jnp.int32, shape, axis)


def exchange_segments(tiles):
    segment = iota(tiles[0].shape, 1) // 32
    a, b, c, d = tiles
    low = segment < 2
    a, c = jnp.where(low, a, pltpu.roll(c, 64, 1)), jnp.where(low, pltpu.roll(a, 64, 1), c)
    b, d = jnp.where(low, b, pltpu.roll(d, 64, 1)), jnp.where(low, pltpu.roll(b, 64, 1), d)
    even = segment % 2 == 0
    a, b = jnp.where(even, a, pltpu.roll(b, 32, 1)), jnp.where(even, pltpu.roll(a, 96, 1), b)
    c, d = jnp.where(even, c, pltpu.roll(d, 32, 1)), jnp.where(even, pltpu.roll(c, 96, 1), d)
    return a, b, c, d


def kernel(nsx, nsy, parts, field_hbm, fx, fy, fz_hbm, recv2, crecv, field, bd_h, bd_l, ux, uy, fz, send1, recv1, bsend,
           brecv, rsend, rrecv, send2, csend, in_s, ux_s, ux_r, uy_s, uy_r, a1_s, a1_r, b1_s, b1_r, b2_s, b2_r, a2_s, a2_r,
           c_s, c_r):
    snaps, xl, yl, nz = field.shape
    cgs = send1.shape[1]
    each = cgs // parts
    bl = bsend.shape[2]
    sx, sy = lax.axis_index("sx"), lax.axis_index("sy")
    z_order, y_order = (2, 1, 3), (2, 1, 3)

    def to_x(i):
        q = lax.rem(sx + i, nsx)
        return q, {"sx": q}

    def to_y(i):
        q = lax.rem(sy + i, nsy)
        return q, {"sy": q}

    def send(src, dst, send_sem, recv_sem, device):
        return pltpu.make_async_remote_copy(src_ref=src, dst_ref=dst, send_sem=send_sem, recv_sem=recv_sem,
                                            device_id=device, device_id_type=MESH)

    def exchange(source, landing, me, peer_of, order, sems, p):
        started = []
        for i in order:
            q, device = peer_of(i)
            started.append(send(source.at[q, p * each:(p + 1) * each], landing.at[me, p * each:(p + 1) * each],
                                sems[0].at[p * 4 + i], sems[1].at[p * 4 + i], device))
            started[-1].start()
        landing[pl.ds(me, 1), p * each:(p + 1) * each] = source[pl.ds(me, 1), p * each:(p + 1) * each]
        return started

    def finish_all(started):
        for copy in started:
            copy.wait()

    loads = [pltpu.make_async_copy(fz_hbm, fz, in_s.at[0])]
    for s in range(snaps):
        loads.append(pltpu.make_async_copy(field_hbm.at[s], field.at[s], in_s.at[1 + s]))
    loads.append(pltpu.make_async_copy(fx, ux.at[sx], in_s.at[1 + snaps]))
    loads.append(pltpu.make_async_copy(fy, uy.at[sy], in_s.at[2 + snaps]))
    for load in loads:
        load.start()

    barrier = pltpu.get_barrier_semaphore()
    for i in z_order:
        pl.semaphore_signal(barrier, inc=1, device_id=to_x(i)[1], device_id_type=MESH)
    for i in y_order:
        pl.semaphore_signal(barrier, inc=1, device_id=to_y(i)[1], device_id_type=MESH)

    spread_r, spread_c = iota((32, 256), 0), iota((32, 256), 1)
    spread = jnp.where((spread_c // 32 == spread_r // 4) & (spread_c % 4 == spread_r % 4), 1.0, 0.0).astype(BF16)
    loads[0].wait()
    lane_x = (iota((nz, 256), 1) // 4) % 8
    for ref, part in zip((bd_h, bd_l), split(fz[...])):
        wide = dot(part, spread, TN)
        for j in range(8):
            ref[j * nz:(j + 1) * nz, :] = jnp.where(lane_x == j, wide, 0.0).astype(BF16)
    bd = (bd_h[...], bd_l[...])

    xo = xl // 8
    for s in range(snaps):
        loads[1 + s].wait()
        snap = field[s].reshape(xo, 8, yl, nz)
        rows = jnp.concatenate([snap[:, j].reshape(xo * yl, nz) for j in range(8)], axis=1)
        packed = dot3(split(rows), bd)
        for t in range(2):
            tiles = [packed[o * yl:(o + 1) * yl, t * 128:(t + 1) * 128] for o in range(xo)]
            for k, tile in enumerate(exchange_segments(tiles)):
                send1[s * 2 + t, k] = tile

    pl.semaphore_wait(barrier, nsx + nsy - 2)
    factor_y = [send(fy, uy.at[sy], uy_s.at[i], uy_r.at[i], to_y(i)[1]) for i in y_order]
    factor_x = [send(fx, ux.at[sx], ux_s.at[i], ux_r.at[i], to_x(i)[1]) for i in z_order]
    for copy in factor_y:
        copy.start()
    a1 = [exchange(send1, recv1, sy, to_y, y_order, (a1_s, a1_r), p) for p in range(parts)]
    for copy in factor_x:
        copy.start()

    finish_all(loads[1 + snaps:] + factor_y)
    uy_all = uy[...].reshape(nsy * yl, uy.shape[2])
    rank2 = uy_all.shape[1]
    uy_p = split(uy_all)
    eye = jnp.where(iota((rank2, rank2), 0) == iota((rank2, rank2), 1), 1.0, 0.0).astype(BF16)
    uy_t = tuple(dot(eye, part, NT).astype(BF16) for part in uy_p)

    b1 = []
    for p in range(parts):
        finish_all(a1[p])
        mine = range(p * each, (p + 1) * each)
        h = jnp.concatenate([recv1[:, g].reshape(nsy * yl, 128) for g in mine], axis=1)
        z = dot3(uy_t, split(h))
        for k, g in enumerate(mine):
            bsend[:, g] = z[:, k * 128:(k + 1) * 128].reshape(nsx, bl, 128)
        b1.append(exchange(bsend, brecv, sx, to_x, z_order, (b1_s, b1_r), p))

    finish_all(factor_x)
    ux_all = ux[...].reshape(nsx * xl, ux.shape[2])
    rank1 = ux_all.shape[1]
    nx = nsx * xl
    wide_x = 4 * nx
    repeat = jnp.where(iota((wide_x, nx), 0) // 4 == iota((wide_x, nx), 1), 1.0, 0.0).astype(BF16)
    ux_pad = jnp.concatenate([ux_all, jnp.zeros((nx, 128 - rank1), F32)], axis=1)
    xe_f = [dot(repeat, part) for part in split(ux_pad)]
    xe = [part.astype(BF16) for part in xe_f]
    same = (iota((wide_x, wide_x), 0) % 4) == (iota((wide_x, wide_x), 1) % 4)
    px = split(jnp.where(same, dot3(xe, xe, NT), 0.0))
    row_c = iota((wide_x, 128), 0) % 4
    wx = [jnp.concatenate([jnp.where(row_c == c, part, 0.0).astype(BF16) for c in range(4)], axis=1) for part in xe_f]

    b2, got = [], []
    for p in range(parts):
        finish_all(b1[p])
        mine = range(p * each, (p + 1) * each)
        got.append(split(jnp.concatenate(
            [brecv[x, p * each:(p + 1) * each].reshape(each * bl, 128) for x in range(nsx)], axis=1)))
        r = dot3(got[p], px)
        for x in range(nsx):
            rsend[x, p * each:(p + 1) * each] = r[:, x * 128:(x + 1) * 128].reshape(each, bl, 128)
        b2.append(exchange(rsend, rrecv, sx, to_x, z_order, (b2_s, b2_r), p))

    third = []
    for p in range(parts):
        core = dot3(got[p], wx)
        for k in range(each):
            g = p * each + k
            for y in range(nsy):
                csend[y, g * 4:(g + 1) * 4, :] = core[k * bl + y * 4:k * bl + (y + 1) * 4, :]
    for i in y_order:
        q, device = to_y(i)
        third.append(send(csend.at[q], crecv.at[sy], c_s.at[i], c_r.at[i], device))
        third[-1].start()
    crecv[pl.ds(sy, 1)] = csend[pl.ds(sy, 1)]

    a2 = []
    for p in range(parts):
        finish_all(b2[p])
        mine = range(p * each, (p + 1) * each)
        r = jnp.concatenate([rrecv[:, g].reshape(rank2, 128) for g in mine], axis=1)
        y = dot3(uy_p, split(r))
        for k, g in enumerate(mine):
            send2[:, g] = y[:, k * 128:(k + 1) * 128].reshape(nsy, yl, 128)
        a2.append(exchange(send2, recv2, sy, to_y, y_order, (a2_s, a2_r), p))
    for started in a2 + [third]:
        finish_all(started)


def finish(recv2, crecv, field, bd_h, bd_l, core_hbm, res_hbm, core_out, res_out, sems):
    snaps, xl, yl, nz = field.shape
    rank1 = core_out.shape[1]
    xo = xl // 8
    bd = (bd_h[...], bd_l[...])
    stores = []
    for s in range(snaps):
        halves = []
        for t in range(2):
            tiles = exchange_segments([recv2[s * 2 + t, k] for k in range(4)])
            halves.append(jnp.concatenate(tiles, axis=0))
        rebuilt = dot3(split(jnp.concatenate(halves, axis=1)), bd, NT)
        for j in range(8):
            for o in range(xo):
                res_out[s, o * 8 + j] = field[s, o * 8 + j] - rebuilt[o * yl:(o + 1) * yl, j * nz:(j + 1) * nz]
        stores.append(pltpu.make_async_copy(res_out.at[s], res_hbm.at[s], sems.at[s]))
        stores[-1].start()

    k = iota((128, 128), 0)
    lane = (k % 4) * 32 + ((k // 4) % 8) * 4 + k // 32
    order = jnp.where(lane == iota((128, 128), 1), 1.0, 0.0).astype(BF16)
    for s in range(snaps):
        got = crecv[s * 2:(s + 1) * 2].reshape(32, 512)
        high, low = split(jnp.concatenate([got[:, c * 128:(c + 1) * 128] for c in range(4)], axis=0))
        core_out[s] = (dot(high, order, TN) + dot(low, order, TN))[:rank1]
    stores.append(pltpu.make_async_copy(core_out, core_hbm, sems.at[snaps]))
    stores[-1].start()
    for store in stores:
        store.wait()


def plain(field, factor_x, factor_y, factor_z):
    highest = lax.Precision.HIGHEST
    inner = jnp.einsum("sxyz,zc->sxyc", field, factor_z, precision=highest)
    inner = jnp.einsum("sxyc,yb->sxbc", inner, factor_y, precision=highest)
    snaps = inner.shape[0]
    rank_one = factor_x.shape[1]
    rank_two = inner.shape[2]
    rank_three = inner.shape[3]
    flat_width = rank_two * rank_three
    partial_core = jnp.einsum("sxbc,xa->sabc", inner, factor_x, precision=highest)
    flat_terms = partial_core.reshape(snaps, rank_one, flat_width)
    core_slice = lax.psum_scatter(flat_terms, ("sx", "sy"), scatter_dimension=2, tiled=True)
    whole_core = lax.all_gather(core_slice, ("sx", "sy"), axis=2, tiled=True)
    kernel = whole_core.reshape(snaps, rank_one, rank_two, rank_three)
    outer = jnp.einsum("sabc,xa->sxbc", kernel, factor_x, precision=highest)
    outer = jnp.einsum("sxbc,yb->sxyc", outer, factor_y, precision=highest)
    outer = jnp.einsum("sxyc,zc->sxyz", outer, factor_z, precision=highest)
    return (core_slice, field - outer)


def local(nsx, nsy, field, factor_x, factor_y, factor_z):
    snaps, xl, yl, nz = field.shape
    rank1, rank2, rank3 = factor_x.shape[1], factor_y.shape[1], factor_z.shape[1]
    n = nsx * nsy
    fits = (nsx == 4 and nsy == 4 and snaps == 2 and rank3 == 32 and xl == 32 and nz == 128 and yl % 24 == 0 and rank2 == 64
            and rank1 <= 128 and rank1 % 8 == 0 and yl <= 64)
    if not fits:
        return plain(field, factor_x, factor_y, factor_z)
    vmem = pl.BlockSpec(memory_space=pltpu.VMEM)
    dma = pltpu.SemaphoreType.DMA
    hbm = pl.BlockSpec(memory_space=pltpu.HBM)
    bl = rank2 // nsx
    a_shape, b_shape, c_shape = (nsy, 4, yl, 128), (nsx, 4, bl, 128), (nsy, 4 * rank2 // n, 512)
    passed = pl.pallas_call(
        functools.partial(kernel, nsx, nsy, PARTS),
        out_shape=(
            jax.ShapeDtypeStruct(a_shape, F32),
            jax.ShapeDtypeStruct(c_shape, F32),
            jax.ShapeDtypeStruct(field.shape, F32),
            jax.ShapeDtypeStruct((8 * nz, 256), BF16),
            jax.ShapeDtypeStruct((8 * nz, 256), BF16),
        ),
        in_specs=[hbm] * 4,
        out_specs=(vmem,) * 5,
        scratch_shapes=[
            pltpu.VMEM((nsx, xl, rank1), F32),
            pltpu.VMEM((nsy, yl, rank2), F32),
            pltpu.VMEM((rank3, nz), F32),
            pltpu.VMEM(a_shape, F32), pltpu.VMEM(a_shape, F32),
            pltpu.VMEM(b_shape, F32), pltpu.VMEM(b_shape, F32),
            pltpu.VMEM(b_shape, F32), pltpu.VMEM(b_shape, F32),
            pltpu.VMEM(a_shape, F32),
            pltpu.VMEM(c_shape, F32),
            dma((snaps + 3,)),
            dma((4,)), dma((4,)), dma((4,)), dma((4,)),
            dma((4 * PARTS,)), dma((4 * PARTS,)), dma((4 * PARTS,)), dma((4 * PARTS,)),
            dma((4 * PARTS,)), dma((4 * PARTS,)), dma((4 * PARTS,)), dma((4 * PARTS,)),
            dma((4,)), dma((4,)),
        ],
        compiler_params=pltpu.CompilerParams(collective_id=0, has_side_effects=True, vmem_limit_bytes=40 * 2**20),
    )(*[pltpu.with_memory_space_constraint(v, pltpu.HBM) for v in (field, factor_x, factor_y, factor_z.T)])
    core_shape = (snaps, rank1, rank2 * rank3 // n)
    return pl.pallas_call(
        finish,
        out_shape=(jax.ShapeDtypeStruct(core_shape, F32), jax.ShapeDtypeStruct(field.shape, F32)),
        in_specs=[vmem] * 5,
        out_specs=(hbm, hbm),
        scratch_shapes=[pltpu.VMEM(core_shape, F32), pltpu.VMEM(field.shape, F32), dma((snaps + 1,))],
        compiler_params=pltpu.CompilerParams(vmem_limit_bytes=40 * 2**20),
    )(*passed)


def solution(mesh):
    in_specs = (P("grp", "sx", "sy", None), P("sx", None), P("sy", None), P())
    out_specs = (P("grp", None, ("sx", "sy")), P("grp", "sx", "sy", None))
    body = functools.partial(local, mesh.shape["sx"], mesh.shape["sy"])
    return jax.shard_map(body, mesh=mesh, in_specs=in_specs, out_specs=out_specs, check_vma=False)
```

time: 26.4 us -> 25.1 us (0.951)
  Pallas kernels: 25.6 us -> 24.2 us
    pallas_call x1, Pallas kernels: 23.6 us -> 22.2 us  [local(): pl.pallas_call(functools.partial(kernel, nsx, nsy, PARTS), out_shape=(jax...]
where the time goes in v3:
time: 25.1 us; the launch traced here: 24.9 us
  Pallas kernels  24.2 us (96%)
  between operations  0.64 us (3%)
    pallas_call x1, Pallas kernels, local(): pl.pallas_call(functools.partial(kernel, nsx, nsy, PARTS), out_shape=(jax...  22.2 us
    pallas_call x1, Pallas kernels, local(): pl.pallas_call(finish, out_shape=(jax.ShapeDtypeStruct(core_shape, F32),...  2 us

profile of v3, /device:TPU:0, one launch (start us, length us, event | category | flops | bytes accessed | tf_op | source)
XLA Modules:
  0.0 24.9 jit_solution(12854560966886801222)
XLA Ops:
  0.6 22.2 %shard_map.59 = (f32[4,4,24,128]{3,2,1,0:T(8,128)S(1)}, f32[4,16,512]{2,1,0:T(8,128)S(1)}, f32[2,32,24,128]{3,2,1,0:T(8,128)S(1)}, bf16[1024,256]{1,0:T(8,128)(2,1)S(1)}, bf16[1024,256]{1,0:T(8,128)(2,1)S(1)}) custom-call(f32[2,32,24,128]{3,2,1,0:T(8,128)} %field_hbm.1, f32[32,96]{1,0:T(8,128)} %fx.1, f32[24,64]{1,0:T(8,128)} %fy.1, f32[32,128]{1,0:T(8,128)} %bitcast.1), custom_call_target="tpu_custom_call" | custom-call | tf_op jit(solution)/shard_map/pallas_call | solution.py:260
  22.9 2.0 %shard_map.60 = (f32[2,96,128]{2,1,0:T(8,128)}, f32[2,32,24,128]{3,2,1,0:T(8,128)}) custom-call(f32[4,4,24,128]{3,2,1,0:T(8,128)S(1)} %get-tuple-element.7.recv2, f32[4,16,512]{2,1,0:T(8,128)S(1)} %get-tuple-element.8.crecv, f32[2,32,24,128]{3,2,1,0:T(8,128)S(1)} %get-tuple-element.9.field, bf16[1024,256]{1,0:T(8,128)(2,1)S(1)} %get-tuple-element.10.bd_h, ...), custom_call_target="tpu_custom_call" | custom-call | tf_op jit(solution)/shard_map/pallas_call | solution.py:289

commit v4 on v3

--- a/solution.py
+++ b/solution.py
@@ -45,7 +45,7 @@
     return a, b, c, d
 
 
-def kernel(nsx, nsy, parts, field_hbm, fx, fy, fz_hbm, recv2, crecv, field, bd_h, bd_l, ux, uy, fz, send1, recv1, bsend,
+def kernel(nsx, nsy, parts, field_hbm, fx, fy, fz_hbm, recv2, crecv, field, bt_h, bt_l, ux, uy, fz, bd_h, bd_l, send1, recv1, bsend,
            brecv, rsend, rrecv, send2, csend, in_s, ux_s, ux_r, uy_s, uy_r, a1_s, a1_r, b1_s, b1_r, b2_s, b2_r, a2_s, a2_r,
            c_s, c_r):
     snaps, xl, yl, nz = field.shape
@@ -67,15 +67,25 @@
         return pltpu.make_async_remote_copy(src_ref=src, dst_ref=dst, send_sem=send_sem, recv_sem=recv_sem,
                                             device_id=device, device_id_type=MESH)
 
-    def exchange(source, landing, me, peer_of, order, sems, p):
-        started = []
-        for i in order:
-            q, device = peer_of(i)
-            started.append(send(source.at[q, p * each:(p + 1) * each], landing.at[me, p * each:(p + 1) * each],
-                                sems[0].at[p * 4 + i], sems[1].at[p * 4 + i], device))
-            started[-1].start()
-        landing[pl.ds(me, 1), p * each:(p + 1) * each] = source[pl.ds(me, 1), p * each:(p + 1) * each]
-        return started
+    def exchange(source, landing, axis, me, order, sems, p):
+        for q in order:
+            part = slice(p * each, (p + 1) * each)
+
+            @pl.when(me != q)
+            def _():
+                send(source.at[q, part], landing.at[me, part], sems[0].at[p * 4 + q], sems[1].at[p * 4 + me], {axis: q}).start()
+
+            @pl.when(me == q)
+            def _():
+                landing[q, part] = source[q, part]
+
+    def arrived(source, landing, axis, me, sems, p):
+        for q in range(4):
+            part = slice(p * each, (p + 1) * each)
+
+            @pl.when(me != q)
+            def _():
+                send(source.at[q, part], landing.at[q, part], sems[0].at[p * 4 + q], sems[1].at[p * 4 + q], {axis: q}).wait()
 
     def finish_all(started):
         for copy in started:
@@ -105,6 +115,12 @@
             ref[j * nz:(j + 1) * nz, :] = jnp.where(lane_x == j, wide, 0.0).astype(BF16)
     bd = (bd_h[...], bd_l[...])
 
+    factor_y = [send(fy, uy.at[sy], uy_s.at[i], uy_r.at[i], to_y(i)[1]) for i in y_order]
+    factor_x = [send(fx, ux.at[sx], ux_s.at[i], ux_r.at[i], to_x(i)[1]) for i in z_order]
+    a1 = (send1, recv1, "sy", sy)
+    b1 = (bsend, brecv, "sx", sx)
+    b2 = (rsend, rrecv, "sx", sx)
+    a2 = (send2, recv2, "sy", sy)
     xo = xl // 8
     for s in range(snaps):
         loads[1 + s].wait()
@@ -114,17 +130,23 @@
         for t in range(2):
             tiles = [packed[o * yl:(o + 1) * yl, t * 128:(t + 1) * 128] for o in range(xo)]
             for k, tile in enumerate(exchange_segments(tiles)):
-                send1[s * 2 + t, k] = tile
-
-    pl.semaphore_wait(barrier, nsx + nsy - 2)
-    factor_y = [send(fy, uy.at[sy], uy_s.at[i], uy_r.at[i], to_y(i)[1]) for i in y_order]
-    factor_x = [send(fx, ux.at[sx], ux_s.at[i], ux_r.at[i], to_x(i)[1]) for i in z_order]
-    for copy in factor_y:
-        copy.start()
-    a1 = [exchange(send1, recv1, sy, to_y, y_order, (a1_s, a1_r), p) for p in range(parts)]
+                send1[t * 2 + s, k] = tile
+        if s == 0:
+            pl.semaphore_wait(barrier, nsx + nsy - 2)
+            for copy in factor_y:
+                copy.start()
+        for p in range(parts):
+            exchange(*a1, (s, 2 + s), (a1_s, a1_r), p)
     for copy in factor_x:
         copy.start()
 
+    spread_t = jnp.where((iota((256, 32), 0) // 32 == iota((256, 32), 1) // 4)
+                         & (iota((256, 32), 0) % 4 == iota((256, 32), 1) % 4), 1.0, 0.0).astype(BF16)
+    row_x = (iota((256, nz), 0) // 4) % 8
+    for ref, part in zip((bt_h, bt_l), split(fz[...])):
+        wide = dot(spread_t, part)
+        for j in range(8):
+            ref[:, j * nz:(j + 1) * nz] = jnp.where(row_x == j, wide, 0.0).astype(BF16)
     finish_all(loads[1 + snaps:] + factor_y)
     uy_all = uy[...].reshape(nsy * yl, uy.shape[2])
     rank2 = uy_all.shape[1]
@@ -132,15 +154,14 @@
     eye = jnp.where(iota((rank2, rank2), 0) == iota((rank2, rank2), 1), 1.0, 0.0).astype(BF16)
     uy_t = tuple(dot(eye, part, NT).astype(BF16) for part in uy_p)
 
-    b1 = []
-    for p in range(parts):
-        finish_all(a1[p])
+    for p in range(parts):
+        arrived(*a1, (a1_s, a1_r), p)
         mine = range(p * each, (p + 1) * each)
         h = jnp.concatenate([recv1[:, g].reshape(nsy * yl, 128) for g in mine], axis=1)
         z = dot3(uy_t, split(h))
         for k, g in enumerate(mine):
             bsend[:, g] = z[:, k * 128:(k + 1) * 128].reshape(nsx, bl, 128)
-        b1.append(exchange(bsend, brecv, sx, to_x, z_order, (b1_s, b1_r), p))
+        exchange(*b1, (0, 1, 3, 2), (b1_s, b1_r), p)
 
     finish_all(factor_x)
     ux_all = ux[...].reshape(nsx * xl, ux.shape[2])
@@ -156,16 +177,16 @@
     row_c = iota((wide_x, 128), 0) % 4
     wx = [jnp.concatenate([jnp.where(row_c == c, part, 0.0).astype(BF16) for c in range(4)], axis=1) for part in xe_f]
 
-    b2, got = [], []
-    for p in range(parts):
-        finish_all(b1[p])
+    got = []
+    for p in range(parts):
+        arrived(*b1, (b1_s, b1_r), p)
         mine = range(p * each, (p + 1) * each)
         got.append(split(jnp.concatenate(
             [brecv[x, p * each:(p + 1) * each].reshape(each * bl, 128) for x in range(nsx)], axis=1)))
         r = dot3(got[p], px)
         for x in range(nsx):
             rsend[x, p * each:(p + 1) * each] = r[:, x * 128:(x + 1) * 128].reshape(each, bl, 128)
-        b2.append(exchange(rsend, rrecv, sx, to_x, z_order, (b2_s, b2_r), p))
+        exchange(*b2, (0, 1, 3, 2), (b2_s, b2_r), p)
 
     third = []
     for p in range(parts):
@@ -180,31 +201,31 @@
         third[-1].start()
     crecv[pl.ds(sy, 1)] = csend[pl.ds(sy, 1)]
 
-    a2 = []
-    for p in range(parts):
-        finish_all(b2[p])
+    for p in range(parts):
+        arrived(*b2, (b2_s, b2_r), p)
         mine = range(p * each, (p + 1) * each)
         r = jnp.concatenate([rrecv[:, g].reshape(rank2, 128) for g in mine], axis=1)
         y = dot3(uy_p, split(r))
         for k, g in enumerate(mine):
             send2[:, g] = y[:, k * 128:(k + 1) * 128].reshape(nsy, yl, 128)
-        a2.append(exchange(send2, recv2, sy, to_y, y_order, (a2_s, a2_r), p))
-    for started in a2 + [third]:
-        finish_all(started)
-
-
-def finish(recv2, crecv, field, bd_h, bd_l, core_hbm, res_hbm, core_out, res_out, sems):
+        exchange(*a2, (0, 1, 2, 3), (a2_s, a2_r), p)
+    for p in range(parts):
+        arrived(*a2, (a2_s, a2_r), p)
+    finish_all(third)
+
+
+def finish(recv2, crecv, field, bt_h, bt_l, core_hbm, res_hbm, core_out, res_out, sems):
     snaps, xl, yl, nz = field.shape
     rank1 = core_out.shape[1]
     xo = xl // 8
-    bd = (bd_h[...], bd_l[...])
+    bt = (bt_h[...], bt_l[...])
     stores = []
     for s in range(snaps):
         halves = []
         for t in range(2):
-            tiles = exchange_segments([recv2[s * 2 + t, k] for k in range(4)])
+            tiles = exchange_segments([recv2[t * 2 + s, k] for k in range(4)])
             halves.append(jnp.concatenate(tiles, axis=0))
-        rebuilt = dot3(split(jnp.concatenate(halves, axis=1)), bd, NT)
+        rebuilt = dot3(split(jnp.concatenate(halves, axis=1)), bt)
         for j in range(8):
             for o in range(xo):
                 res_out[s, o * 8 + j] = field[s, o * 8 + j] - rebuilt[o * yl:(o + 1) * yl, j * nz:(j + 1) * nz]
@@ -215,7 +236,7 @@
     lane = (k % 4) * 32 + ((k // 4) % 8) * 4 + k // 32
     order = jnp.where(lane == iota((128, 128), 1), 1.0, 0.0).astype(BF16)
     for s in range(snaps):
-        got = crecv[s * 2:(s + 1) * 2].reshape(32, 512)
+        got = jnp.concatenate([crecv[s], crecv[2 + s]], axis=0)
         high, low = split(jnp.concatenate([got[:, c * 128:(c + 1) * 128] for c in range(4)], axis=0))
         core_out[s] = (dot(high, order, TN) + dot(low, order, TN))[:rank1]
     stores.append(pltpu.make_async_copy(core_out, core_hbm, sems.at[snaps]))
@@ -263,8 +284,8 @@
             jax.ShapeDtypeStruct(a_shape, F32),
             jax.ShapeDtypeStruct(c_shape, F32),
             jax.ShapeDtypeStruct(field.shape, F32),
-            jax.ShapeDtypeStruct((8 * nz, 256), BF16),
-            jax.ShapeDtypeStruct((8 * nz, 256), BF16),
+            jax.ShapeDtypeStruct((256, 8 * nz), BF16),
+            jax.ShapeDtypeStruct((256, 8 * nz), BF16),
         ),
         in_specs=[hbm] * 4,
         out_specs=(vmem,) * 5,
@@ -272,6 +293,7 @@
             pltpu.VMEM((nsx, xl, rank1), F32),
             pltpu.VMEM((nsy, yl, rank2), F32),
             pltpu.VMEM((rank3, nz), F32),
+            pltpu.VMEM((8 * nz, 256), BF16), pltpu.VMEM((8 * nz, 256), BF16),
             pltpu.VMEM(a_shape, F32), pltpu.VMEM(a_shape, F32),
             pltpu.VMEM(b_shape, F32), pltpu.VMEM(b_shape, F32),
             pltpu.VMEM(b_shape, F32), pltpu.VMEM(b_shape, F32),

time: 25.1 us -> 24.4 us (0.972)
  Pallas kernels: 24.2 us -> 23.5 us
    pallas_call x1, Pallas kernels: 2 us -> 1.56 us  [local(): pl.pallas_call(finish, out_shape=(jax.ShapeDtypeStruct(core_shape, F32),...]
    pallas_call x1, Pallas kernels: 22.2 us -> 22 us  [local(): pl.pallas_call(functools.partial(kernel, nsx, nsy, PARTS), out_shape=(jax...]
where the time goes in v4:
time: 24.4 us; the launch traced here: 24.2 us
  Pallas kernels  23.5 us (96%)
  between operations  0.64 us (3%)
    pallas_call x1, Pallas kernels, local(): pl.pallas_call(functools.partial(kernel, nsx, nsy, PARTS), out_shape=(jax...  22 us
    pallas_call x1, Pallas kernels, local(): pl.pallas_call(finish, out_shape=(jax.ShapeDtypeStruct(core_shape, F32),...  1.56 us

profile of v4, /device:TPU:0, one launch (start us, length us, event | category | flops | bytes accessed | tf_op | source)
XLA Modules:
  0.0 24.2 jit_solution(9841326665036696858)
XLA Ops:
  0.6 22.0 %shard_map.59 = (f32[4,4,24,128]{3,2,1,0:T(8,128)S(1)}, f32[4,16,512]{2,1,0:T(8,128)S(1)}, f32[2,32,24,128]{3,2,1,0:T(8,128)S(1)}, bf16[256,1024]{1,0:T(8,128)(2,1)S(1)}, bf16[256,1024]{1,0:T(8,128)(2,1)S(1)}) custom-call(f32[2,32,24,128]{3,2,1,0:T(8,128)} %field_hbm.1, f32[32,96]{1,0:T(8,128)} %fx.1, f32[24,64]{1,0:T(8,128)} %fy.1, f32[32,128]{1,0:T(8,128)} %bitcast.1), custom_call_target="tpu_custom_call" | custom-call | tf_op jit(solution)/shard_map/pallas_call | solution.py:281
  22.6 1.6 %shard_map.60 = (f32[2,96,128]{2,1,0:T(8,128)}, f32[2,32,24,128]{3,2,1,0:T(8,128)}) custom-call(f32[4,4,24,128]{3,2,1,0:T(8,128)S(1)} %get-tuple-element.7.recv2, f32[4,16,512]{2,1,0:T(8,128)S(1)} %get-tuple-element.8.crecv, f32[2,32,24,128]{3,2,1,0:T(8,128)S(1)} %get-tuple-element.9.field, bf16[256,1024]{1,0:T(8,128)(2,1)S(1)} %get-tuple-element.10.bt_h, ...), custom_call_target="tpu_custom_call" | custom-call | tf_op jit(solution)/shard_map/pallas_call | solution.py:311
